TPU v7x, 32 devices: a whole 2x2x4 slice. The times are simulated.
32 devices in a mesh: dom: 32 (over z, y, x, core).
Axes of the slice: x: 2, y: 2, z: 4, core: 2. Of those that a mesh axis runs over, the one named last changes fastest.
Arguments:
- dofs_start: float32 [9, 56, 4096], P(None, None, 'dom'), may hold values from -6 to 6
- star_matrix: float32 [3, 9, 9, 4096], P(None, None, None, 'dom'), may hold values from -2 to 2
- flux_local: float32 [4, 9, 9, 4096], P(None, None, None, 'dom'), may hold values from -2 to 2
- flux_neighbour: float32 [4, 9, 9, 4096], P(None, None, None, 'dom'), may hold values from -2 to 2
- derivative: float32 [3, 56, 56], replicated, may hold values from -0.75 to 0.75
- face_project: float32 [4, 56, 21], replicated, may hold values from -0.75 to 0.75
- face_lift: float32 [4, 21, 56], replicated, may hold values from -0.625 to 0.625
- face_turn: float32 [3, 21, 21], replicated, may hold values from -1.25 to 1.25
- cluster: int32 [4096], P('dom'), may hold values from 0 to 1, as said below
- face_neighbour: int32 [4, 4096], P(None, 'dom'), may hold values from 0 to 640, as said below
- orientation: int32 [4, 4096], P(None, 'dom'), may hold values from 0 to 2
- send_list: int32 [4, 1024], P(None, 'dom'), may hold values from 0 to 511, as said below
Outputs:
- dofs_end: float32 [9, 56, 4096], P(None, None, 'dom')
Inputs may be any that keep to these rules, and one draw needn't show every extreme that they name: On each partition the elements of cluster 0 come before those of cluster 1; a partition holds 32 to 96 elements of cluster 0, and some partition exactly 96. `face_neighbour`: A code v < 512 is face v // 128 of local element v % 128; 512 + k * 32 + s is slot s of block k of the face table; 640 is the outer boundary. Face pairs are symmetric. `send_list`: each partition's row k holds 32 of its local face codes, each face in at most one slot of all rows.
All inputs are finite; a program needn't handle non-finite values.
Results may differ from a plain program's by a relative error of at most 0.0003.
Values sent between devices are 32-bit elements; how exact they have to be, the bound alone decides.
A program may use at most 64 MiB of HBM per device.

v0:
```python
import functools
import math

import jax
import jax.numpy as jnp
from jax import lax
from jax.experimental import pallas as pl
from jax.experimental.pallas import tpu as pltpu
from jax.sharding import PartitionSpec as P

ORDER = 6
time_step = 0.5
reach_offsets = (1, -1, 2, -2)
MESH = pl.DeviceIdType.MESH
LANES = 128
f32, bf16 = jnp.float32, jnp.bfloat16
groups = ((0, 1, 2, 3), (4, 5, 6, 7), (8,))


def weight(power, lower, upper):
    return (upper ** (power + 1) - lower ** (power + 1)) / math.factorial(power + 1)


def split(x):
    high = x.astype(bf16)
    return high, (x - high.astype(f32)).astype(bf16)


def stacked(x):
    high, low = split(x)
    return jnp.concatenate([high, high, low], axis=0)


def place(pieces, blocks):
    out = []
    for block in range(blocks):
        total = None
        for x, offset, width in pieces:
            if offset >= (block + 1) * LANES or offset + width <= block * LANES:
                continue
            moved = pltpu.roll(x, offset % LANES, axis=1) if offset % LANES else x
            lane = lax.broadcasted_iota(jnp.int32, x.shape, 1) + block * LANES
            moved = jnp.where((lane >= offset) & (lane < offset + width), moved, 0.0)
            total = moved if total is None else total + moved
        out.append(total)
    return out[0] if blocks == 1 else jnp.concatenate(out, axis=1)


def three(x, width):
    high = x.astype(bf16).astype(f32)
    low = x - high
    blocks = -(-3 * width // LANES)
    whole = place([(high, 0, width), (low, width, width), (high, 2 * width, width)], blocks)
    return whole.astype(bf16)


def pad_rows(x, rows):
    if x.shape[0] == rows:
        return x
    return jnp.concatenate([x, jnp.zeros((rows - x.shape[0], x.shape[1]), x.dtype)], axis=0)


def kernel(
    peers,
    dofs, star, flux_l, flux_n, deriv, proj, lift, turn, cluster, codes, orient, sends,
    out,
    square, a_slope, a_vol, a_proj, a_lift, a_turn,
    hot, hot_send, code_row,
    shifted, integral, late, faces, table, outside, turned, fluxes, sent, got,
    send_sem, recv_sem,
):
    me = lax.axis_index("dom")
    nq, nb, ne = dofs.shape
    nf = proj.shape[2]
    slot = sends.shape[1]
    fr = 24
    kb = 64

    barrier = pltpu.get_barrier_semaphore()
    for offset in reach_offsets:
        pl.semaphore_signal(
            barrier, inc=1, device_id=(lax.rem(me + offset + peers, peers),), device_id_type=MESH
        )

    square[...] = jnp.zeros_like(square)
    for d in range(3):
        square[0:nb, 0:nb] = deriv[d]
        a_vol[d * nb:(d + 1) * nb, :] = three(square[0:nb, :], kb)[:, :3 * kb].astype(f32)
        flipped = -jnp.transpose(square[...])
        a_slope[d * nb:(d + 1) * nb, :] = three(flipped[0:nb, :], kb)[:, :3 * kb].astype(f32)
    square[...] = jnp.zeros_like(square)
    for i in range(4):
        square[0:nb, 0:nf] = proj[i]
        flipped = jnp.transpose(square[...])
        a_proj[i * fr:(i + 1) * fr, :] = three(flipped[0:fr, :], kb)[:, :3 * kb].astype(f32)
    square[...] = jnp.zeros_like(square)
    for i in range(4):
        square[i * fr:i * fr + nf, 0:nb] = lift[i]
    flipped = jnp.transpose(square[...])
    a_lift[...] = three(flipped[0:nb, :], 4 * fr)[:, :12 * fr].astype(f32)
    square[...] = jnp.zeros_like(square)
    for h in range(3):
        square[0:nf, 0:nf] = turn[h]
        flipped = jnp.transpose(square[...])
        a_turn[h * fr:(h + 1) * fr, :] = three(flipped[0:fr, :], 32)[:, :96].astype(f32)

    for i in range(4):
        for start in range(0, 640, 128):
            number = lax.broadcasted_iota(jnp.int32, (128, ne), 0) + start
            same = number == codes[i:i + 1, :]
            hot[start:start + 128, i * ne:(i + 1) * ne] = jnp.where(same, 1.0, 0.0).astype(bf16)
    code_row[...] = jnp.zeros_like(code_row)
    code_row[0:4, 0:slot] = sends[...]
    wanted = code_row[0:1, :]
    for k in range(1, 4):
        wanted = wanted + pltpu.roll(code_row[...], k * slot, axis=1)[k:k + 1, :]
    for start in range(0, 512, 128):
        number = lax.broadcasted_iota(jnp.int32, (128, ne), 0) + start
        hot_send[start:start + 128, :] = jnp.where(number == wanted, 1.0, 0.0).astype(bf16)

    table[...] = jnp.zeros_like(table)
    for q in range(nq):
        out[q] = dofs[q]

    def products(lhs, values, emit):
        at = 0
        while at < len(values):
            pair = values[at:at + 2]
            rhs = [stacked(pad_rows(v, kb)) for v in pair]
            rhs = rhs[0] if len(rhs) == 1 else jnp.concatenate(rhs, axis=1)
            got_ = jnp.dot(lhs, rhs, preferred_element_type=f32)
            for j in range(len(pair)):
                emit(at + j, got_[:, j * LANES:(j + 1) * LANES])
            at += 2

    def star_apply(buffer, ps):
        acc = [None] * len(ps)
        for q in range(nq):
            for d in range(3):
                s = shifted[buffer, q, d * nb:(d + 1) * nb, :]
                for j, p in enumerate(ps):
                    term = star[d, p, q:q + 1, :] * s
                    acc[j] = term if acc[j] is None else acc[j] + term
        return acc

    lane = lax.broadcasted_iota(jnp.int32, (nb, LANES), 1)

    def stage(s, carry):
        slope_lhs = a_slope[...].astype(bf16)

        def keep(buffer, first):
            def emit(index, product):
                shifted[buffer, first + index] = product
            return emit

        for ps in groups:
            values = [out[p] for p in ps]
            for p, v in zip(ps, values):
                integral[p] = weight(0, 0.0, time_step) * v
                late[s, p] = weight(0, time_step, 2 * time_step) * v
            products(slope_lhs, values, keep(0, ps[0]))
        for power in range(1, ORDER):
            buffer = (power - 1) % 2
            for ps in groups:
                values = star_apply(buffer, ps)
                for p, v in zip(ps, values):
                    integral[p] += weight(power, 0.0, time_step) * v
                    late[s, p] += weight(power, time_step, 2 * time_step) * v
                if power < ORDER - 1:
                    products(slope_lhs, values, keep(1 - buffer, ps[0]))

        slow = (jnp.broadcast_to(cluster[...], (nb, LANES)) != 0) & (s == 1)
        values = []
        for q in range(nq):
            values.append(jnp.where(slow, late[0, q], integral[q]))

        def emit_faces(q, product):
            faces[q] = product
            for i in range(4):
                table[q * fr:(q + 1) * fr, i * ne:(i + 1) * ne] = product[i * fr:(i + 1) * fr]
        products(a_proj[...].astype(bf16), values, emit_faces)

        high, low = split(table[:, 0:4 * ne])
        chosen = jnp.dot(high, hot_send[...], preferred_element_type=f32) + jnp.dot(
            low, hot_send[...], preferred_element_type=f32
        )
        for k in range(4):
            packed = None
            for j in range(4):
                rows = chosen[j * nb:(j + 1) * nb]
                shift = ((j - k) % 4) * slot
                rows = pltpu.roll(rows, shift, axis=1) if shift else rows
                packed = rows if packed is None else jnp.where(lane >= j * slot, rows, packed)
            sent[s, k] = packed

        @pl.when(s == 0)
        def _():
            pl.semaphore_wait(barrier, 4)

        copies = []
        for k, offset in enumerate(reach_offsets):
            copy = pltpu.make_async_remote_copy(
                src_ref=sent.at[s, k],
                dst_ref=got.at[s, k],
                send_sem=send_sem.at[s, k],
                recv_sem=recv_sem.at[s, k],
                device_id=(lax.rem(me + offset + peers, peers),),
                device_id_type=MESH,
            )
            copy.start()
            copies.append(copy)

        products(a_vol[...].astype(bf16), values, keep(0, 0))
        outside[...] = jnp.dot(high, hot[0:4 * ne, :], preferred_element_type=f32) + jnp.dot(
            low, hot[0:4 * ne, :], preferred_element_type=f32
        )
        for ps in groups:
            for p, v in zip(ps, star_apply(0, ps)):
                out[p] += v
        for i in range(4):
            acc = [None] * nq
            for q in range(nq):
                trace = faces[q, i * fr:(i + 1) * fr, :]
                for p in range(nq):
                    term = flux_l[i, p, q:q + 1, :] * trace
                    acc[p] = term if acc[p] is None else acc[p] + term
            for p in range(nq):
                fluxes[p, i * fr:(i + 1) * fr, :] = acc[p]

        for copy in copies:
            copy.wait()
        for j in range(4):
            rows = None
            for k in range(4):
                block = got[s, k]
                shift = ((k - j) % 4) * slot
                block = pltpu.roll(block, shift, axis=1) if shift else block
                rows = block if rows is None else jnp.where(lane >= k * slot, block, rows)
            table[j * nb:(j + 1) * nb, 4 * ne:5 * ne] = rows
        high, low = split(table[:, 4 * ne:5 * ne])
        outside[...] += jnp.dot(high, hot[4 * ne:5 * ne, :], preferred_element_type=f32) + jnp.dot(
            low, hot[4 * ne:5 * ne, :], preferred_element_type=f32
        )

        turn_lhs = a_turn[...].astype(bf16)
        for q in range(nq):
            rhs = stacked(pad_rows(outside[q * fr:(q + 1) * fr, :], 32))
            product = jnp.dot(turn_lhs, rhs, preferred_element_type=f32)
            for i in range(4):
                which = jnp.broadcast_to(orient[i:i + 1, :], (fr, LANES))
                h0, h1, h2 = (
                    product[h * fr:(h + 1) * fr, i * ne:(i + 1) * ne] for h in range(3)
                )
                turned[q, i * fr:(i + 1) * fr, :] = jnp.where(
                    which == 0, h0, jnp.where(which == 1, h1, h2)
                )
        for i in range(4):
            acc = [fluxes[p, i * fr:(i + 1) * fr, :] for p in range(nq)]
            for q in range(nq):
                trace = turned[q, i * fr:(i + 1) * fr, :]
                for p in range(nq):
                    acc[p] = acc[p] + flux_n[i, p, q:q + 1, :] * trace
            for p in range(nq):
                fluxes[p, i * fr:(i + 1) * fr, :] = acc[p]
        lift_lhs = a_lift[...].astype(bf16)
        for at in range(0, nq, 2):
            pair = list(range(at, min(at + 2, nq)))
            rhs = [stacked(fluxes[p]) for p in pair]
            rhs = rhs[0] if len(rhs) == 1 else jnp.concatenate(rhs, axis=1)
            surface = jnp.dot(lift_lhs, rhs, preferred_element_type=f32)
            for j, p in enumerate(pair):
                out[p] -= surface[:, j * LANES:(j + 1) * LANES]
        return carry

    lax.fori_loop(0, 2, stage, 0)


def per_device(*args):
    peers = lax.axis_size("dom")
    dofs = args[0]
    nq, nb, ne = dofs.shape
    cluster = args[8].reshape(1, ne)
    args = args[:8] + (cluster,) + args[9:]
    vmem = pl.BlockSpec(memory_space=pltpu.VMEM)
    return pl.pallas_call(
        functools.partial(kernel, peers),
        out_shape=jax.ShapeDtypeStruct(dofs.shape, dofs.dtype),
        in_specs=[vmem] * 12,
        out_specs=vmem,
        scratch_shapes=[
            pltpu.VMEM((128, 128), f32),
            pltpu.VMEM((168, 192), f32),
            pltpu.VMEM((168, 192), f32),
            pltpu.VMEM((96, 192), f32),
            pltpu.VMEM((56, 288), f32),
            pltpu.VMEM((72, 96), f32),
            pltpu.VMEM((640, 512), bf16),
            pltpu.VMEM((512, 128), bf16),
            pltpu.VMEM((8, 128), jnp.int32),
            pltpu.VMEM((2, 9, 168, 128), f32),
            pltpu.VMEM((9, 56, 128), f32),
            pltpu.VMEM((2, 9, 56, 128), f32),
            pltpu.VMEM((9, 96, 128), f32),
            pltpu.VMEM((224, 640), f32),
            pltpu.VMEM((224, 512), f32),
            pltpu.VMEM((9, 96, 128), f32),
            pltpu.VMEM((9, 96, 128), f32),
            pltpu.VMEM((2, 4, 56, 128), f32),
            pltpu.VMEM((2, 4, 56, 128), f32),
            pltpu.SemaphoreType.DMA((2, 4)),
            pltpu.SemaphoreType.DMA((2, 4)),
        ],
        compiler_params=pltpu.CompilerParams(
            collective_id=0, has_side_effects=True, vmem_limit_bytes=40 * 1024 * 1024
        ),
        cost_estimate=pl.CostEstimate(
            flops=400_000_000, bytes_accessed=2_000_000, transcendentals=0
        ),
    )(*args)


def solution(mesh):
    return jax.shard_map(
        per_device,
        mesh=mesh,
        in_specs=(
            P(None, None, "dom"),
            P(None, None, None, "dom"),
            P(None, None, None, "dom"),
            P(None, None, None, "dom"),
            P(),
            P(),
            P(),
            P(),
            P("dom"),
            P(None, "dom"),
            P(None, "dom"),
            P(None, "dom"),
        ),
        out_specs=P(None, None, "dom"),
        check_vma=False,
    )
```

profile of v0, /device:TPU:0, one launch (start us, length us, event | category | flops | bytes accessed | tf_op | source)
XLA Modules:
  0.0 28.4 jit_solution(8973524345351554587)
XLA Ops:
  0.0 0.0 copy-start.9
  0.0 0.8 %copy.17.lift = f32[4,21,56]{2,1,0:T(8,128)S(1)} copy(f32[4,21,56]{2,0,1:T(4,128)} %param.18) | data formatting | bytes 37632 | tf_op args[6]
  0.8 0.9 %copy.16.proj = f32[4,56,21]{2,1,0:T(8,128)S(1)} copy(f32[4,56,21]{1,0,2:T(4,128)} %param.17) | data formatting | bytes 37632 | tf_op args[5]
  1.7 0.0 copy-done.9
  1.7 0.0 copy-start.7
  1.8 0.9 %copy-done.7 = f32[4,9,9,128]{3,0,2,1:T(4,128)S(1)} copy-done((f32[4,9,9,128]{3,0,2,1:T(4,128)S(1)}, f32[4,9,9,128]{3,0,2,1:T(4,128)}, u32[]{:S(2)}) %copy-start.7) | copy-done | bytes 165912
  2.6 0.0 copy-start.8
  2.7 0.9 %copy-done.8 = f32[4,9,9,128]{3,0,2,1:T(4,128)S(1)} copy-done((f32[4,9,9,128]{3,0,2,1:T(4,128)S(1)}, f32[4,9,9,128]{3,0,2,1:T(4,128)}, u32[]{:S(2)}) %copy-start.8) | copy-done | bytes 165912
  3.6 0.0 copy-start
  3.6 0.0 copy-start.1
  3.6 0.0 copy-start.2
  3.6 0.0 copy-start.3
  3.6 0.0 copy-start.4
  3.6 0.0 copy-start.5
  3.6 0.0 copy-start.6
  3.6 0.9 %copy-done = f32[9,56,128]{2,1,0:T(8,128)S(1)} copy-done((f32[9,56,128]{2,1,0:T(8,128)S(1)}, f32[9,56,128]{2,1,0:T(8,128)}, u32[]{:S(2)}) %copy-start) | copy-done | bytes 258072
  4.5 0.1 copy-done.1
  4.6 0.0 copy-done.2
  4.6 0.0 copy-done.3
  4.6 0.0 copy-done.4
  4.6 0.0 copy-done.5
  4.6 0.0 copy-done.6
  4.6 23.1 %shard_map.118 = f32[9,56,128]{2,1,0:T(8,128)S(1)} custom-call(f32[9,56,128]{2,1,0:T(8,128)S(1)} %copy-done, f32[3,9,9,128]{3,2,1,0:T(8,128)S(1)} %copy.13.star, f32[4,9,9,128]{3,2,1,0:T(8,128)S(1)} %copy.14.flux_l, f32[4,9,9,128]{3,2,1,0:T(8,128)S(1)} %copy.15.flux_n, f32[3,56,56]{2,1,0:T(8,128)S(1)} %copy-done.1, f32[4,56,21]{2,1,0:T(8,128)S(1)} %copy.16.proj, ...), custom_call_target="tpu_custom_call" | custom-call | flops 400000000 | bytes 2000000 | tf_op jit(solution)/shard_map/pallas_call | solution.py:285
  27.7 0.7 %copy.19 = f32[9,56,128]{2,1,0:T(8,128)} copy(f32[9,56,128]{2,1,0:T(8,128)S(1)} %shard_map.118) | data formatting | bytes 516096
  (3 shorter events, 0.1 us)
Async XLA Ops:
  0.0 1.7 %copy-start.9 = (f32[3,9,9,128]{3,0,2,1:T(4,128)S(1)}, f32[3,9,9,128]{3,0,2,1:T(4,128)}, u32[]{:S(2)}) copy-start(f32[3,9,9,128]{3,0,2,1:T(4,128)} %param.13) | copy-start | bytes 373252
  1.7 0.9 %copy-start.7 = (f32[4,9,9,128]{3,0,2,1:T(4,128)S(1)}, f32[4,9,9,128]{3,0,2,1:T(4,128)}, u32[]{:S(2)}) copy-start(f32[4,9,9,128]{3,0,2,1:T(4,128)} %param.14) | copy-start | bytes 497668
  2.6 0.9 %copy-start.8 = (f32[4,9,9,128]{3,0,2,1:T(4,128)S(1)}, f32[4,9,9,128]{3,0,2,1:T(4,128)}, u32[]{:S(2)}) copy-start(f32[4,9,9,128]{3,0,2,1:T(4,128)} %param.15) | copy-start | bytes 497668
  3.6 0.9 %copy-start = (f32[9,56,128]{2,1,0:T(8,128)S(1)}, f32[9,56,128]{2,1,0:T(8,128)}, u32[]{:S(2)}) copy-start(f32[9,56,128]{2,1,0:T(8,128)} %dofs.1) | copy-start | bytes 774148
  3.6 1.0 %copy-start.1 = (f32[3,56,56]{2,1,0:T(8,128)S(1)}, f32[3,56,56]{2,1,0:T(8,128)}, u32[]{:S(2)}) copy-start(f32[3,56,56]{2,1,0:T(8,128)} %deriv.1) | copy-start | bytes 112900
  3.6 1.0 %copy-start.2 = (f32[3,21,21]{2,1,0:T(8,128)S(1)}, f32[3,21,21]{2,1,0:T(8,128)}, u32[]{:S(2)}) copy-start(f32[3,21,21]{2,1,0:T(8,128)} %turn.1) | copy-start | bytes 15880
  3.6 1.0 %copy-start.3 = (s32[4,128]{1,0:T(4,128)S(1)}, s32[4,128]{1,0:T(4,128)}, u32[]{:S(2)}) copy-start(s32[4,128]{1,0:T(4,128)} %codes.1) | copy-start | bytes 6148
  3.6 1.0 %copy-start.4 = (s32[4,128]{1,0:T(4,128)S(1)}, s32[4,128]{1,0:T(4,128)}, u32[]{:S(2)}) copy-start(s32[4,128]{1,0:T(4,128)} %orient.1) | copy-start | bytes 6148
  3.6 1.0 %copy-start.5 = (s32[4,32]{1,0:T(4,128)S(1)}, s32[4,32]{1,0:T(4,128)}, u32[]{:S(2)}) copy-start(s32[4,32]{1,0:T(4,128)} %sends.1) | copy-start | bytes 1540
  3.6 1.0 %copy-start.6 = (s32[128]{0:T(128)S(1)}, s32[128]{0:T(128)}, u32[]{:S(2)}) copy-start(s32[128]{0:T(128)} %param.20) | copy-start | bytes 1540
where the time goes:
time: 28.7 us; the launch traced here: 28.4 us
  Pallas kernels  23.1 us (80%)
  local copies, waits for them, and re-layouts  5.22 us (18%)
    pallas_call x1, Pallas kernels, per_device(): pl.pallas_call(functools.partial(kernel, peers), out_shape=jax.ShapeDtype...  23.1 us
    unnamed x26, local copies, waits for them, and re-layouts  5.22 us

commit v1 on v0

--- a/solution.py
+++ b/solution.py
@@ -62,6 +62,14 @@
 
 def kernel(
     peers,
+    *refs,
+):
+    far, out, near, loaded = refs[:12], refs[12], refs[13:25], refs[25]
+    run(peers, far, near, loaded, *near, out, *refs[26:])
+
+
+def run(
+    peers, far, near, loaded,
     dofs, star, flux_l, flux_n, deriv, proj, lift, turn, cluster, codes, orient, sends,
     out,
     square, a_slope, a_vol, a_proj, a_lift, a_turn,
@@ -71,7 +79,7 @@
 ):
     me = lax.axis_index("dom")
     nq, nb, ne = dofs.shape
-    nf = proj.shape[2]
+    nf = proj.shape[0]
     slot = sends.shape[1]
     fr = 24
     kb = 64
@@ -82,27 +90,40 @@
             barrier, inc=1, device_id=(lax.rem(me + offset + peers, peers),), device_id_type=MESH
         )
 
+    loads = [pltpu.make_async_copy(far[n], near[n], loaded.at[n]) for n in range(12)]
+    for n in (4, 5, 6, 7, 8, 9, 10, 11, 0, 1, 2, 3):
+        loads[n].start()
+    for n in range(4, 12):
+        loads[n].wait()
+
     square[...] = jnp.zeros_like(square)
     for d in range(3):
-        square[0:nb, 0:nb] = deriv[d]
-        a_vol[d * nb:(d + 1) * nb, :] = three(square[0:nb, :], kb)[:, :3 * kb].astype(f32)
+        row = (d % 2) * kb
+        square[row:row + nb, 0:nb] = deriv[d]
+        a_vol[d * nb:(d + 1) * nb, :] = three(square[row:row + nb, :], kb)[:, :3 * kb].astype(f32)
+        if d == 0:
+            continue
         flipped = -jnp.transpose(square[...])
-        a_slope[d * nb:(d + 1) * nb, :] = three(flipped[0:nb, :], kb)[:, :3 * kb].astype(f32)
+        for e in ((0, 1) if d == 1 else (2,)):
+            part = flipped[0:nb, :]
+            part = pltpu.roll(part, kb, axis=1) if e % 2 else part
+            a_slope[e * nb:(e + 1) * nb, :] = three(part, kb)[:, :3 * kb].astype(f32)
     square[...] = jnp.zeros_like(square)
     for i in range(4):
-        square[0:nb, 0:nf] = proj[i]
-        flipped = jnp.transpose(square[...])
-        a_proj[i * fr:(i + 1) * fr, :] = three(flipped[0:fr, :], kb)[:, :3 * kb].astype(f32)
+        square[0:nf, 0:nb] = proj[:, i, :]
+        a_proj[i * fr:(i + 1) * fr, :] = three(square[0:fr, :], kb)[:, :3 * kb].astype(f32)
     square[...] = jnp.zeros_like(square)
     for i in range(4):
-        square[i * fr:i * fr + nf, 0:nb] = lift[i]
+        square[i * fr:i * fr + nf, 0:nb] = lift[:, i, :]
     flipped = jnp.transpose(square[...])
     a_lift[...] = three(flipped[0:nb, :], 4 * fr)[:, :12 * fr].astype(f32)
     square[...] = jnp.zeros_like(square)
     for h in range(3):
-        square[0:nf, 0:nf] = turn[h]
-        flipped = jnp.transpose(square[...])
-        a_turn[h * fr:(h + 1) * fr, :] = three(flipped[0:fr, :], 32)[:, :96].astype(f32)
+        square[h * 32:h * 32 + nf, 0:nf] = turn[h]
+    flipped = jnp.transpose(square[...])[0:fr, :]
+    for h in range(3):
+        part = pltpu.roll(flipped, LANES - h * 32, axis=1) if h else flipped
+        a_turn[h * fr:(h + 1) * fr, :] = three(part, 32)[:, :96].astype(f32)
 
     for i in range(4):
         for start in range(0, 640, 128):
@@ -119,6 +140,8 @@
         hot_send[start:start + 128, :] = jnp.where(number == wanted, 1.0, 0.0).astype(bf16)
 
     table[...] = jnp.zeros_like(table)
+    loads[0].wait()
+    loads[1].wait()
     for q in range(nq):
         out[q] = dofs[q]
 
@@ -139,7 +162,7 @@
             for d in range(3):
                 s = shifted[buffer, q, d * nb:(d + 1) * nb, :]
                 for j, p in enumerate(ps):
-                    term = star[d, p, q:q + 1, :] * s
+                    term = star[p, q, d:d + 1, :] * s
                     acc[j] = term if acc[j] is None else acc[j] + term
         return acc
 
@@ -195,6 +218,8 @@
 
         @pl.when(s == 0)
         def _():
+            loads[2].wait()
+            loads[3].wait()
             pl.semaphore_wait(barrier, 4)
 
         copies = []
@@ -222,7 +247,7 @@
             for q in range(nq):
                 trace = faces[q, i * fr:(i + 1) * fr, :]
                 for p in range(nq):
-                    term = flux_l[i, p, q:q + 1, :] * trace
+                    term = flux_l[p, q, i:i + 1, :] * trace
                     acc[p] = term if acc[p] is None else acc[p] + term
             for p in range(nq):
                 fluxes[p, i * fr:(i + 1) * fr, :] = acc[p]
@@ -259,7 +284,7 @@
             for q in range(nq):
                 trace = turned[q, i * fr:(i + 1) * fr, :]
                 for p in range(nq):
-                    acc[p] = acc[p] + flux_n[i, p, q:q + 1, :] * trace
+                    acc[p] = acc[p] + flux_n[p, q, i:i + 1, :] * trace
             for p in range(nq):
                 fluxes[p, i * fr:(i + 1) * fr, :] = acc[p]
         lift_lhs = a_lift[...].astype(bf16)
@@ -280,14 +305,18 @@
     dofs = args[0]
     nq, nb, ne = dofs.shape
     cluster = args[8].reshape(1, ne)
-    args = args[:8] + (cluster,) + args[9:]
+    across = [jnp.transpose(a, (1, 2, 0, 3)) for a in args[1:4]]
+    proj, lift = jnp.transpose(args[5], (2, 0, 1)), jnp.transpose(args[6], (1, 0, 2))
+    args = (dofs, *across, args[4], proj, lift, args[7], cluster, *args[9:])
     vmem = pl.BlockSpec(memory_space=pltpu.VMEM)
     return pl.pallas_call(
         functools.partial(kernel, peers),
         out_shape=jax.ShapeDtypeStruct(dofs.shape, dofs.dtype),
-        in_specs=[vmem] * 12,
+        in_specs=[pl.BlockSpec(memory_space=pl.ANY)] * 12,
         out_specs=vmem,
         scratch_shapes=[
+            *(pltpu.VMEM(a.shape, a.dtype) for a in args),
+            pltpu.SemaphoreType.DMA((12,)),
             pltpu.VMEM((128, 128), f32),
             pltpu.VMEM((168, 192), f32),
             pltpu.VMEM((168, 192), f32),
@@ -311,7 +340,7 @@
             pltpu.SemaphoreType.DMA((2, 4)),
         ],
         compiler_params=pltpu.CompilerParams(
-            collective_id=0, has_side_effects=True, vmem_limit_bytes=40 * 1024 * 1024
+            collective_id=0, has_side_effects=True, vmem_limit_bytes=60 * 1024 * 1024
         ),
         cost_estimate=pl.CostEstimate(
             flops=400_000_000, bytes_accessed=2_000_000, transcendentals=0

time: 28.7 us -> 26.2 us (0.913)
  local copies, waits for them, and re-layouts: 5.22 us -> 1.66 us
  Pallas kernels: 23.1 us -> 24.4 us
    unnamed x26 -> x1, local copies, waits for them, and re-layouts: 5.22 us -> 1.66 us
    pallas_call x1, Pallas kernels: 23.1 us -> 24.4 us  [per_device(): pl.pallas_call(functools.partial(kernel, peers), out_shape=jax.ShapeDtype...]
where the time goes in v1:
time: 26.2 us; the launch traced here: 26 us
  Pallas kernels  24.4 us (93%)
  local copies, waits for them, and re-layouts  1.66 us (6%)
    pallas_call x1, Pallas kernels, per_device(): pl.pallas_call(functools.partial(kernel, peers), out_shape=jax.ShapeDtype...  24.4 us
    unnamed x1, local copies, waits for them, and re-layouts  1.66 us

profile of v1, /device:TPU:0, one launch (start us, length us, event | category | flops | bytes accessed | tf_op | source)
XLA Modules:
  0.0 26.0 jit_solution(13252807418253160531)
XLA Ops:
  0.0 24.4 %shard_map.118 = f32[9,56,128]{2,1,0:T(8,128)} custom-call(f32[9,56,128]{2,1,0:T(8,128)} %refs_0_.1, f32[9,9,3,128]{3,2,1,0:T(4,128)} %bitcast.6, f32[9,9,4,128]{3,2,1,0:T(4,128)} %bitcast.7, f32[9,9,4,128]{3,2,1,0:T(4,128)} %bitcast.8, f32[3,56,56]{2,1,0:T(8,128)} %refs_4_.1, f32[21,4,56]{2,1,0:T(4,128)} %bitcast.9, f32[21,4,56]{2,1,0:T(4,128)} %bitcast.10, ...), custom_call_target="tpu_custom_call" | custom-call | flops 400000000 | bytes 2000000 | tf_op jit(solution)/shard_map/pallas_call | solution.py:312
  24.4 1.7 %copy.14 = f32[9,56,128]{2,1,0:T(8,128)} copy(f32[9,56,128]{2,1,0:T(8,128)} %shard_map.118) | data formatting | bytes 516096
